TPU v7x, 32 devices: a whole 2x2x4 slice. The times are simulated.
32 devices in a mesh: seg: 16 (over z, y, x), samp: 2 (over core).
Axes of the slice: x: 2, y: 2, z: 4, core: 2. Of those that a mesh axis runs over, the one named last changes fastest.
Arguments:
- rigidity_diagonal_cells: bfloat16 [512, 128, 128], P('seg')
- rigidity_lower_cells: bfloat16 [512, 128, 128], P('seg'), may hold values from -0.5 to 0.5
- inverse_diagonal_cells: bfloat16 [512, 128, 128], P('seg')
- bedding_rigidity_per_unknown: float32 [512, 128], P('seg'), may hold values from 0.3 to 2
- bedding_regime: int32 [512], P('seg'), may hold values from 0 to 2
- dilation_push_per_kelvin: float32 [512, 128], P('seg'), may hold values from 1 to 16
- heat_shape_functions: bfloat16 [512, 512], P('seg'), may hold values from -0.25 to 0.25
- sampled_shape_weights: bfloat16 [64, 512], P('samp'), may hold values from -6 to 6
- joined_segment_table: int32 [16, 2], P('seg'), may hold values from 0 to 15
- joint_rigidity: float32 [16, 2], P('seg'), may hold values from 1.2 to 3.6
Outputs:
- displacement: float32 [64, 512, 128], P('samp', 'seg')
- kl_grad: float32 [512], replicated
Inputs may be any that keep to these rules, and one draw needn't show every extreme that they name: `joined_segment_table`: every entry names a segment.
All inputs are finite; a program needn't handle non-finite values.
Results may differ from a plain program's by a relative error of at most 0.013.
Values may be sent and summed in bfloat16 or wider, within the bound.
A program may use at most 64 MiB of HBM per device.

v0:
```python
import math

import jax
import jax.numpy as jnp
from jax import lax
from jax.sharding import PartitionSpec as P

STEPS = 4


def shifted(value, axis, steps):
    count = lax.axis_size(axis)
    first, last = (max(0, -steps), min(count, count - steps))
    return lax.ppermute(value, axis, [(source, source + steps) for source in range(first, last)])


def stiffness(
    field_round, rigidity_diagonal_cells, rigidity_lower_cells, joined_segment_table, joint_rigidity
):
    own_term = jnp.einsum(
        "sjb,jab->sja", field_round, rigidity_diagonal_cells, preferred_element_type=jnp.float32
    )
    upward = jnp.einsum(
        "sjb,jba->sja", field_round, rigidity_lower_cells, preferred_element_type=jnp.float32
    ).astype(jnp.bfloat16)
    below_rim = shifted(field_round[:, -1:, :], "seg", 1)
    above_rim = shifted(upward[:, :1, :], "seg", -1)
    interfaces = lax.all_gather(field_round[:, :1, :], "seg", axis=1, tiled=True)
    lower_field = jnp.concatenate([below_rim, field_round[:, :-1]], axis=1)
    below_term = jnp.einsum(
        "sjb,jab->sja", lower_field, rigidity_lower_cells, preferred_element_type=jnp.float32
    )
    upper_term = jnp.concatenate([upward[:, 1:], above_rim], axis=1).astype(jnp.float32)
    result = own_term + below_term + upper_term
    partner = jnp.take(interfaces, joined_segment_table[0], axis=1).astype(jnp.float32)
    own_interface = field_round[:, 0:1, :].astype(jnp.float32)
    spring = jnp.sum(joint_rigidity[0][None, :, None] * (own_interface - partner), axis=1)
    return result.at[:, 0, :].add(spring)


def ballast(state, bedding_rigidity_per_unknown, bedding_regime):
    code = bedding_regime[None, :, None]
    stiff = bedding_rigidity_per_unknown[None]
    magnitude = 1.0 + jnp.abs(state)
    slide = jnp.tanh(state)
    force = jnp.where(
        code == 0, stiff * state, jnp.where(code == 1, stiff * state / magnitude, stiff * slide)
    )
    tangent = jnp.where(
        code == 0,
        stiff + 0.0 * state,
        jnp.where(code == 1, stiff / (magnitude * magnitude), stiff * (1.0 - slide * slide)),
    )
    return (force, tangent)


def blockwise(inverse_diagonal_cells, field_round):
    return jnp.einsum(
        "jab,sjb->sja", inverse_diagonal_cells, field_round, preferred_element_type=jnp.float32
    )


def body(
    rigidity_diagonal_cells,
    rigidity_lower_cells,
    inverse_diagonal_cells,
    bedding_rigidity_per_unknown,
    bedding_regime,
    dilation_push_per_kelvin,
    heat_shape_functions,
    sampled_shape_weights,
    joined_segment_table,
    joint_rigidity,
):
    samples_here = sampled_shape_weights.shape[0]
    blocks_here = rigidity_diagonal_cells.shape[0]
    width = rigidity_diagonal_cells.shape[1]
    shape_functions = heat_shape_functions.shape[1]
    complete_shape_functions = heat_shape_functions.astype(jnp.float32)
    heat_distribution = jnp.dot(
        sampled_shape_weights, heat_shape_functions.T, preferred_element_type=jnp.float32
    )
    heat_driven_source = dilation_push_per_kelvin[None] * heat_distribution[:, :, None]
    state = jnp.zeros((samples_here, blocks_here, width), jnp.float32)
    grad_total = jnp.zeros((shape_functions,), jnp.float32)
    for iteration in range(STEPS):
        state_round = state.astype(jnp.bfloat16)
        force, tangent = ballast(state, bedding_rigidity_per_unknown, bedding_regime)
        residual_vector = (
            heat_driven_source
            - stiffness(
                state_round,
                rigidity_diagonal_cells,
                rigidity_lower_cells,
                joined_segment_table,
                joint_rigidity,
            )
            - force
        )
        initial_newton_step = blockwise(
            inverse_diagonal_cells, residual_vector.astype(jnp.bfloat16)
        )
        second = (
            residual_vector
            - stiffness(
                initial_newton_step.astype(jnp.bfloat16),
                rigidity_diagonal_cells,
                rigidity_lower_cells,
                joined_segment_table,
                joint_rigidity,
            )
            - tangent * initial_newton_step
        )
        state = (
            state
            + initial_newton_step
            + blockwise(inverse_diagonal_cells, second.astype(jnp.bfloat16))
        )
        adjoint = jnp.einsum(
            "sja,jab->sjb",
            state.astype(jnp.bfloat16),
            inverse_diagonal_cells,
            preferred_element_type=jnp.float32,
        )
        weighted = jnp.sum(jnp.sum(dilation_push_per_kelvin[None] * adjoint, axis=2), axis=0)
        partial_value = jnp.dot(weighted, complete_shape_functions, precision=lax.Precision.HIGHEST)
        grad_total = grad_total + lax.psum(partial_value, ("seg", "samp"))
    every_block_list = blocks_here * lax.axis_size("seg")
    all_samples = samples_here * lax.axis_size("samp")
    scale = math.sqrt(shape_functions / (every_block_list * all_samples * width))
    return (state, grad_total * scale)


def solution(mesh):
    placed = (
        P("seg", None, None),
        P("seg", None, None),
        P("seg", None, None),
        P("seg", None),
        P("seg"),
        P("seg", None),
        P("seg", None),
        P("samp", None),
        P("seg", None),
        P("seg", None),
    )
    return jax.shard_map(
        body, mesh=mesh, in_specs=placed, out_specs=(P("samp", "seg", None), P()), check_vma=False
    )
```

profile of v0, /device:TPU:0, one launch (start us, length us, event | category | flops | bytes accessed | tf_op | source)
XLA Modules:
  0.0 459.6 jit_solution(1154479130879753834)
XLA Ops:
  0.7 5.0 %collective-permute-start = (bf16[32,1,128]{2,0,1:T(8,128)(2,1)S(1)}, bf16[32,1,128]{2,0,1:T(8,128)(2,1)S(1)}, u32[]{:S(2)}, u32[]{:S(2)}) collective-permute-start(bf16[32,1,128]{2,0,1:T(8,128)(2,1)S(1)} %slice.302), channel_id=1, source_target_pairs={{0,2},{2,4},{4,6},{6,8},{8,10},{10,12},{12,14},{14,16},{16,18},{18... | collective-permute-start | bytes 24584 | tf_op jit(solution)/shard_map/ppermute | solution.py:14
  17.5 5.1 %collective-permute-start.2 = (bf16[32,1,128]{2,0,1:T(8,128)(2,1)}, bf16[32,1,128]{2,0,1:T(8,128)(2,1)}, u32[]{:S(2)}, u32[]{:S(2)}) collective-permute-start(bf16[32,1,128]{2,0,1:T(8,128)(2,1)} %get-tuple-element.125), channel_id=1, source_target_pairs={{0,2},{2,4},{4,6},{6,8},{8,10},{10,12},{12,14},{14,16},{16,18},{18... | collective-permute-start | bytes 24584 | tf_op jit(solution)/shard_map/ppermute | solution.py:14
  22.6 41.2 %all_gather.22 = bf16[32,16,128]{2,0,1:T(8,128)(2,1)} all-gather(bf16[32,1,128]{2,0,1:T(8,128)(2,1)S(1)} %get-tuple-element.124), channel_id=1, replica_groups=mesh['seg'=16,'samp'=2] {'seg'}, dimensions={1}, use_global_device_ids=true | all-gather | bytes 139264 | tf_op jit(solution)/shard_map/all_gather | solution.py:28
  67.5 4.1 collective-permute-done.3
  73.0 1.5 fusion.133
  76.7 1.5 fusion.141
  78.3 2.6 collective-permute-start.4
  80.9 38.5 %all_gather.23 = bf16[32,16,128]{2,0,1:T(8,128)(2,1)} all-gather(bf16[32,1,128]{2,0,1:T(8,128)(2,1)S(1)} %get-tuple-element.121), channel_id=1, replica_groups=mesh['seg'=16,'samp'=2] {'seg'}, dimensions={1}, use_global_device_ids=true | all-gather | bytes 139264 | tf_op jit(solution)/shard_map/all_gather | solution.py:28
  122.9 4.1 collective-permute-done.5
  129.1 1.5 fusion.134
  133.8 5.4 %collective-permute-start.6 = (bf16[32,1,128]{2,0,1:T(8,128)(2,1)}, bf16[32,1,128]{2,0,1:T(8,128)(2,1)}, u32[]{:S(2)}, u32[]{:S(2)}) collective-permute-start(bf16[32,1,128]{2,0,1:T(8,128)(2,1)} %get-tuple-element.119), channel_id=1, source_target_pairs={{0,2},{2,4},{4,6},{6,8},{8,10},{10,12},{12,14},{14,16},{16,18},{18... | collective-permute-start | bytes 24584 | tf_op jit(solution)/shard_map/ppermute | solution.py:14
  139.2 38.5 %all_gather.24 = bf16[32,16,128]{2,0,1:T(8,128)(2,1)} all-gather(bf16[32,1,128]{2,0,1:T(8,128)(2,1)S(1)} %get-tuple-element.118), channel_id=1, replica_groups=mesh['seg'=16,'samp'=2] {'seg'}, dimensions={1}, use_global_device_ids=true | all-gather | bytes 139264 | tf_op jit(solution)/shard_map/all_gather | solution.py:28
  181.2 4.1 collective-permute-done.7
  187.4 1.6 fusion.135
  191.1 1.5 fusion.143
  193.3 5.4 %collective-permute-start.8 = (bf16[32,1,128]{2,0,1:T(8,128)(2,1)}, bf16[32,1,128]{2,0,1:T(8,128)(2,1)}, u32[]{:S(2)}, u32[]{:S(2)}) collective-permute-start(bf16[32,1,128]{2,0,1:T(8,128)(2,1)} %get-tuple-element.116), channel_id=1, source_target_pairs={{0,2},{2,4},{4,6},{6,8},{8,10},{10,12},{12,14},{14,16},{16,18},{18... | collective-permute-start | bytes 24584 | tf_op jit(solution)/shard_map/ppermute | solution.py:14
  198.7 38.5 %all_gather.25 = bf16[32,16,128]{2,0,1:T(8,128)(2,1)} all-gather(bf16[32,1,128]{2,0,1:T(8,128)(2,1)S(1)} %get-tuple-element.115), channel_id=1, replica_groups=mesh['seg'=16,'samp'=2] {'seg'}, dimensions={1}, use_global_device_ids=true | all-gather | bytes 139264 | tf_op jit(solution)/shard_map/all_gather | solution.py:28
  240.7 4.1 collective-permute-done.9
  246.9 1.5 fusion.136
  251.6 5.4 %collective-permute-start.10 = (bf16[32,1,128]{2,0,1:T(8,128)(2,1)}, bf16[32,1,128]{2,0,1:T(8,128)(2,1)}, u32[]{:S(2)}, u32[]{:S(2)}) collective-permute-start(bf16[32,1,128]{2,0,1:T(8,128)(2,1)} %get-tuple-element.113), channel_id=1, source_target_pairs={{0,2},{2,4},{4,6},{6,8},{8,10},{10,12},{12,14},{14,16},{16,18},{18... | collective-permute-start | bytes 24584 | tf_op jit(solution)/shard_map/ppermute | solution.py:14
  257.0 38.5 %all_gather.26 = bf16[32,16,128]{2,0,1:T(8,128)(2,1)} all-gather(bf16[32,1,128]{2,0,1:T(8,128)(2,1)S(1)} %get-tuple-element.112), channel_id=1, replica_groups=mesh['seg'=16,'samp'=2] {'seg'}, dimensions={1}, use_global_device_ids=true | all-gather | bytes 139264 | tf_op jit(solution)/shard_map/all_gather | solution.py:28
  299.3 3.9 collective-permute-done.11
  305.2 1.6 fusion.137
  308.9 1.5 fusion.145
  311.1 5.4 %collective-permute-start.12 = (bf16[32,1,128]{2,0,1:T(8,128)(2,1)}, bf16[32,1,128]{2,0,1:T(8,128)(2,1)}, u32[]{:S(2)}, u32[]{:S(2)}) collective-permute-start(bf16[32,1,128]{2,0,1:T(8,128)(2,1)} %get-tuple-element.110), channel_id=1, source_target_pairs={{0,2},{2,4},{4,6},{6,8},{8,10},{10,12},{12,14},{14,16},{16,18},{18... | collective-permute-start | bytes 24584 | tf_op jit(solution)/shard_map/ppermute | solution.py:14
  316.5 38.5 %all_gather.27 = bf16[32,16,128]{2,0,1:T(8,128)(2,1)} all-gather(bf16[32,1,128]{2,0,1:T(8,128)(2,1)S(1)} %get-tuple-element.109), channel_id=1, replica_groups=mesh['seg'=16,'samp'=2] {'seg'}, dimensions={1}, use_global_device_ids=true | all-gather | bytes 139264 | tf_op jit(solution)/shard_map/all_gather | solution.py:28
  358.5 4.2 collective-permute-done.13
  364.8 1.5 fusion.138
  368.8 4.8 %collective-permute-start.14 = (bf16[32,1,128]{2,0,1:T(8,128)(2,1)S(1)}, bf16[32,1,128]{2,0,1:T(8,128)(2,1)S(1)}, u32[]{:S(2)}, u32[]{:S(2)}) collective-permute-start(bf16[32,1,128]{2,0,1:T(8,128)(2,1)S(1)} %get-tuple-element.107), channel_id=1, source_target_pairs={{0,2},{2,4},{4,6},{6,8},{8,10},{10,12},{12,14},{14,16},{16,18},{18... | collective-permute-start | bytes 24584 | tf_op jit(solution)/shard_map/ppermute | solution.py:14
  373.7 36.2 %all_gather.28 = bf16[32,16,128]{2,0,1:T(8,128)(2,1)S(1)} all-gather(bf16[32,1,128]{2,0,1:T(8,128)(2,1)S(1)} %get-tuple-element.106), channel_id=1, replica_groups=mesh['seg'=16,'samp'=2] {'seg'}, dimensions={1}, use_global_device_ids=true | all-gather | bytes 139264 | tf_op jit(solution)/shard_map/all_gather | solution.py:28
  412.5 4.1 collective-permute-done.15
  421.3 37.7 %psum.34 = f32[512]{0:T(512)S(1)} all-reduce(f32[512]{0:T(512)S(1)} %add_add_fusion), channel_id=1, replica_groups=mesh['seg'=16,'samp'=2] {'seg','samp'}, use_global_device_ids=true, to_apply=%region_9.11 | all-reduce | flops 512 | bytes 4096 | tf_op jit(solution)/shard_map/psum | solution.py:127
  (226 shorter events, 69.4 us)
Async XLA Ops:
  0.6 5.0 %copy-start = (bf16[32,128,128]{2,1,0:T(8,128)(2,1)S(1)}, bf16[32,128,128]{2,1,0:T(8,128)(2,1)}, u32[]{:S(2)}) copy-start(bf16[32,128,128]{2,1,0:T(8,128)(2,1)} %param.29) | copy-start | bytes 3145732
  0.6 8.1 %copy-start.1 = (bf16[32,128,128]{2,1,0:T(8,128)(2,1)S(1)}, bf16[32,128,128]{2,1,0:T(8,128)(2,1)}, u32[]{:S(2)}) copy-start(bf16[32,128,128]{2,1,0:T(8,128)(2,1)} %param.28) | copy-start | bytes 3145732
  0.7 10.5 %collective-permute-start = (bf16[32,1,128]{2,0,1:T(8,128)(2,1)S(1)}, bf16[32,1,128]{2,0,1:T(8,128)(2,1)S(1)}, u32[]{:S(2)}, u32[]{:S(2)}) collective-permute-start(bf16[32,1,128]{2,0,1:T(8,128)(2,1)S(1)} %slice.302), channel_id=1, source_target_pairs={{0,2},{2,4},{4,6},{6,8},{8,10},{10,12},{12,14},{14,16},{16,18},{18... | collective-permute-start | bytes 24584 | tf_op jit(solution)/shard_map/ppermute | solution.py:14
  6.1 5.7 %collective-permute-start.1 = (bf16[32,1,128]{2,0,1:T(8,128)(2,1)S(1)}, bf16[32,1,128]{2,0,1:T(8,128)(2,1)S(1)}, u32[]{:S(2)}, u32[]{:S(2)}) collective-permute-start(bf16[32,1,128]{2,0,1:T(8,128)(2,1)S(1)} %slice.366), channel_id=1, source_target_pairs={{2,0},{4,2},{6,4},{8,6},{10,8},{12,10},{14,12},{16,14},{18,16},{20... | collective-permute-start | bytes 24584 | tf_op jit(solution)/shard_map/ppermute | solution.py:14
  14.3 53.1 %copy-start.7 = (bf16[32,32,128]{2,0,1:T(8,128)(2,1)}, bf16[32,32,128]{2,0,1:T(8,128)(2,1)S(1)}, u32[]{:S(2)}) copy-start(bf16[32,32,128]{2,0,1:T(8,128)(2,1)S(1)} %convert_bitcast_fusion) | copy-start | bytes 786436
  17.5 50.0 %collective-permute-start.2 = (bf16[32,1,128]{2,0,1:T(8,128)(2,1)}, bf16[32,1,128]{2,0,1:T(8,128)(2,1)}, u32[]{:S(2)}, u32[]{:S(2)}) collective-permute-start(bf16[32,1,128]{2,0,1:T(8,128)(2,1)} %get-tuple-element.125), channel_id=1, source_target_pairs={{0,2},{2,4},{4,6},{6,8},{8,10},{10,12},{12,14},{14,16},{16,18},{18... | collective-permute-start | bytes 24584 | tf_op jit(solution)/shard_map/ppermute | solution.py:14
  66.0 5.5 %collective-permute-start.3 = (bf16[32,1,128]{2,0,1:T(8,128)(2,1)S(1)}, bf16[32,1,128]{2,0,1:T(8,128)(2,1)S(1)}, u32[]{:S(2)}, u32[]{:S(2)}) collective-permute-start(bf16[32,1,128]{2,0,1:T(8,128)(2,1)S(1)} %slice.371), channel_id=1, source_target_pairs={{2,0},{4,2},{6,4},{8,6},{10,8},{12,10},{14,12},{16,14},{18,16},{20... | collective-permute-start | bytes 24584 | tf_op jit(solution)/shard_map/ppermute | solution.py:14
  67.4 5.5 %copy-start.4 = (f32[32,32,128]{2,0,1:T(8,128)S(1)}, f32[32,32,128]{2,0,1:T(8,128)}, u32[]{:S(2)}) copy-start(f32[32,32,128]{2,0,1:T(8,128)} %copy-done.3) | copy-start | bytes 1572868
  67.5 5.5 %copy-start.6 = (f32[32,32,128]{2,1,0:T(8,128)S(1)}, f32[32,32,128]{2,1,0:T(8,128)}, u32[]{:S(2)}) copy-start(f32[32,32,128]{2,1,0:T(8,128)} %copy-done.5) | copy-start | bytes 1572868
  78.3 44.6 %collective-permute-start.4 = (bf16[32,1,128]{2,0,1:T(8,128)(2,1)}, bf16[32,1,128]{2,0,1:T(8,128)(2,1)}, u32[]{:S(2)}, u32[]{:S(2)}) collective-permute-start(bf16[32,1,128]{2,0,1:T(8,128)(2,1)} %get-tuple-element.122), channel_id=1, source_target_pairs={{0,2},{2,4},{4,6},{6,8},{8,10},{10,12},{12,14},{14,16},{16,18},{18... | collective-permute-start | bytes 24584 | tf_op jit(solution)/shard_map/ppermute | solution.py:14
  121.5 5.5 %collective-permute-start.5 = (bf16[32,1,128]{2,0,1:T(8,128)(2,1)S(1)}, bf16[32,1,128]{2,0,1:T(8,128)(2,1)S(1)}, u32[]{:S(2)}, u32[]{:S(2)}) collective-permute-start(bf16[32,1,128]{2,0,1:T(8,128)(2,1)S(1)} %slice.377), channel_id=1, source_target_pairs={{2,0},{4,2},{6,4},{8,6},{10,8},{12,10},{14,12},{16,14},{18,16},{20... | collective-permute-start | bytes 24584 | tf_op jit(solution)/shard_map/ppermute | solution.py:14
  122.9 5.5 %copy-start.24 = (f32[32,32,128]{2,0,1:T(8,128)S(1)}, f32[32,32,128]{2,0,1:T(8,128)}, u32[]{:S(2)}) copy-start(f32[32,32,128]{2,0,1:T(8,128)} %get-tuple-element.129) | copy-start | bytes 1572868
  133.8 47.4 %collective-permute-start.6 = (bf16[32,1,128]{2,0,1:T(8,128)(2,1)}, bf16[32,1,128]{2,0,1:T(8,128)(2,1)}, u32[]{:S(2)}, u32[]{:S(2)}) collective-permute-start(bf16[32,1,128]{2,0,1:T(8,128)(2,1)} %get-tuple-element.119), channel_id=1, source_target_pairs={{0,2},{2,4},{4,6},{6,8},{8,10},{10,12},{12,14},{14,16},{16,18},{18... | collective-permute-start | bytes 24584 | tf_op jit(solution)/shard_map/ppermute | solution.py:14
  179.8 5.5 %collective-permute-start.7 = (bf16[32,1,128]{2,0,1:T(8,128)(2,1)S(1)}, bf16[32,1,128]{2,0,1:T(8,128)(2,1)S(1)}, u32[]{:S(2)}, u32[]{:S(2)}) collective-permute-start(bf16[32,1,128]{2,0,1:T(8,128)(2,1)S(1)} %slice.383), channel_id=1, source_target_pairs={{2,0},{4,2},{6,4},{8,6},{10,8},{12,10},{14,12},{16,14},{18,16},{20... | collective-permute-start | bytes 24584 | tf_op jit(solution)/shard_map/ppermute | solution.py:14
  181.2 5.5 %copy-start.19 = (f32[32,32,128]{2,0,1:T(8,128)S(1)}, f32[32,32,128]{2,0,1:T(8,128)}, u32[]{:S(2)}) copy-start(f32[32,32,128]{2,0,1:T(8,128)} %copy-done.18) | copy-start | bytes 1572868
  181.2 5.5 %copy-start.25 = (f32[32,32,128]{2,0,1:T(8,128)S(1)}, f32[32,32,128]{2,0,1:T(8,128)}, u32[]{:S(2)}) copy-start(f32[32,32,128]{2,0,1:T(8,128)} %get-tuple-element.129) | copy-start | bytes 1572868
  181.2 5.5 %copy-start.50 = (f32[32,32,128]{2,0,1:T(8,128)S(1)}, f32[32,32,128]{2,0,1:T(8,128)}, u32[]{:S(2)}) copy-start(f32[32,32,128]{2,0,1:T(8,128)} %get-tuple-element.131) | copy-start | bytes 1572868
  193.3 47.4 %collective-permute-start.8 = (bf16[32,1,128]{2,0,1:T(8,128)(2,1)}, bf16[32,1,128]{2,0,1:T(8,128)(2,1)}, u32[]{:S(2)}, u32[]{:S(2)}) collective-permute-start(bf16[32,1,128]{2,0,1:T(8,128)(2,1)} %get-tuple-element.116), channel_id=1, source_target_pairs={{0,2},{2,4},{4,6},{6,8},{8,10},{10,12},{12,14},{14,16},{16,18},{18... | collective-permute-start | bytes 24584 | tf_op jit(solution)/shard_map/ppermute | solution.py:14
  239.3 5.5 %collective-permute-start.9 = (bf16[32,1,128]{2,0,1:T(8,128)(2,1)S(1)}, bf16[32,1,128]{2,0,1:T(8,128)(2,1)S(1)}, u32[]{:S(2)}, u32[]{:S(2)}) collective-permute-start(bf16[32,1,128]{2,0,1:T(8,128)(2,1)S(1)} %slice.389), channel_id=1, source_target_pairs={{2,0},{4,2},{6,4},{8,6},{10,8},{12,10},{14,12},{16,14},{18,16},{20... | collective-permute-start | bytes 24584 | tf_op jit(solution)/shard_map/ppermute | solution.py:14
  240.7 5.5 %copy-start.47 = (f32[32,32,128]{2,0,1:T(8,128)S(1)}, f32[32,32,128]{2,0,1:T(8,128)}, u32[]{:S(2)}) copy-start(f32[32,32,128]{2,0,1:T(8,128)} %get-tuple-element.133) | copy-start | bytes 1572868
  251.6 47.7 %collective-permute-start.10 = (bf16[32,1,128]{2,0,1:T(8,128)(2,1)}, bf16[32,1,128]{2,0,1:T(8,128)(2,1)}, u32[]{:S(2)}, u32[]{:S(2)}) collective-permute-start(bf16[32,1,128]{2,0,1:T(8,128)(2,1)} %get-tuple-element.113), channel_id=1, source_target_pairs={{0,2},{2,4},{4,6},{6,8},{8,10},{10,12},{12,14},{14,16},{16,18},{18... | collective-permute-start | bytes 24584 | tf_op jit(solution)/shard_map/ppermute | solution.py:14
  297.6 5.5 %collective-permute-start.11 = (bf16[32,1,128]{2,0,1:T(8,128)(2,1)S(1)}, bf16[32,1,128]{2,0,1:T(8,128)(2,1)S(1)}, u32[]{:S(2)}, u32[]{:S(2)}) collective-permute-start(bf16[32,1,128]{2,0,1:T(8,128)(2,1)S(1)} %slice.395), channel_id=1, source_target_pairs={{2,0},{4,2},{6,4},{8,6},{10,8},{12,10},{14,12},{16,14},{18,16},{20... | collective-permute-start | bytes 24584 | tf_op jit(solution)/shard_map/ppermute | solution.py:14
  299.2 5.3 %copy-start.21 = (f32[32,32,128]{2,0,1:T(8,128)S(1)}, f32[32,32,128]{2,0,1:T(8,128)}, u32[]{:S(2)}) copy-start(f32[32,32,128]{2,0,1:T(8,128)} %copy-done.20) | copy-start | bytes 1572868
  299.2 5.3 %copy-start.48 = (f32[32,32,128]{2,0,1:T(8,128)S(1)}, f32[32,32,128]{2,0,1:T(8,128)}, u32[]{:S(2)}) copy-start(f32[32,32,128]{2,0,1:T(8,128)} %get-tuple-element.133) | copy-start | bytes 1572868
  299.2 5.3 %copy-start.51 = (f32[32,32,128]{2,0,1:T(8,128)S(1)}, f32[32,32,128]{2,0,1:T(8,128)}, u32[]{:S(2)}) copy-start(f32[32,32,128]{2,0,1:T(8,128)} %get-tuple-element.135) | copy-start | bytes 1572868
  311.1 47.4 %collective-permute-start.12 = (bf16[32,1,128]{2,0,1:T(8,128)(2,1)}, bf16[32,1,128]{2,0,1:T(8,128)(2,1)}, u32[]{:S(2)}, u32[]{:S(2)}) collective-permute-start(bf16[32,1,128]{2,0,1:T(8,128)(2,1)} %get-tuple-element.110), channel_id=1, source_target_pairs={{0,2},{2,4},{4,6},{6,8},{8,10},{10,12},{12,14},{14,16},{16,18},{18... | collective-permute-start | bytes 24584 | tf_op jit(solution)/shard_map/ppermute | solution.py:14
  357.1 5.6 %collective-permute-start.13 = (bf16[32,1,128]{2,0,1:T(8,128)(2,1)S(1)}, bf16[32,1,128]{2,0,1:T(8,128)(2,1)S(1)}, u32[]{:S(2)}, u32[]{:S(2)}) collective-permute-start(bf16[32,1,128]{2,0,1:T(8,128)(2,1)S(1)} %slice.401), channel_id=1, source_target_pairs={{2,0},{4,2},{6,4},{8,6},{10,8},{12,10},{14,12},{16,14},{18,16},{20... | collective-permute-start | bytes 24584 | tf_op jit(solution)/shard_map/ppermute | solution.py:14
  358.5 5.6 %copy-start.45 = (f32[32,32,128]{2,0,1:T(8,128)S(1)}, f32[32,32,128]{2,0,1:T(8,128)}, u32[]{:S(2)}) copy-start(f32[32,32,128]{2,0,1:T(8,128)} %get-tuple-element.137) | copy-start | bytes 1572868
  368.8 43.7 %collective-permute-start.14 = (bf16[32,1,128]{2,0,1:T(8,128)(2,1)S(1)}, bf16[32,1,128]{2,0,1:T(8,128)(2,1)S(1)}, u32[]{:S(2)}, u32[]{:S(2)}) collective-permute-start(bf16[32,1,128]{2,0,1:T(8,128)(2,1)S(1)} %get-tuple-element.107), channel_id=1, source_target_pairs={{0,2},{2,4},{4,6},{6,8},{8,10},{10,12},{12,14},{14,16},{16,18},{18... | collective-permute-start | bytes 24584 | tf_op jit(solution)/shard_map/ppermute | solution.py:14
  411.1 5.5 %collective-permute-start.15 = (bf16[32,1,128]{2,0,1:T(8,128)(2,1)S(1)}, bf16[32,1,128]{2,0,1:T(8,128)(2,1)S(1)}, u32[]{:S(2)}, u32[]{:S(2)}) collective-permute-start(bf16[32,1,128]{2,0,1:T(8,128)(2,1)S(1)} %slice.407), channel_id=1, source_target_pairs={{2,0},{4,2},{6,4},{8,6},{10,8},{12,10},{14,12},{16,14},{18,16},{20... | collective-permute-start | bytes 24584 | tf_op jit(solution)/shard_map/ppermute | solution.py:14
  412.5 4.8 %copy-start.23 = (f32[32,32,128]{2,0,1:T(8,128)S(1)}, f32[32,32,128]{2,0,1:T(8,128)}, u32[]{:S(2)}) copy-start(f32[32,32,128]{2,0,1:T(8,128)} %copy-done.22) | copy-start | bytes 1572868
  412.5 4.8 %copy-start.46 = (f32[32,32,128]{2,0,1:T(8,128)S(1)}, f32[32,32,128]{2,0,1:T(8,128)}, u32[]{:S(2)}) copy-start(f32[32,32,128]{2,0,1:T(8,128)} %get-tuple-element.137) | copy-start | bytes 1572868
  (44 other events, 98.0 us)
where the time goes:
time: 462 us; the launch traced here: 460 us
  blocking collectives  307 us (66%)
  starting transfers between devices  49.6 us (11%)
  matrix products  43.6 us (9%)
  waiting for transfers between devices  29.1 us (6%)
  local copies, waits for them, and re-layouts  22.6 us (5%)
  other arithmetic  5.63 us (1%)
    all_gather x7, blocking collectives, stiffness(): lax.all_gather(field_round[:, :1, :], 'seg', axis=1, tiled=True)  270 us
    ppermute x16, starting transfers between devices, shifted(): lax.ppermute(value, axis, [(source, source + steps) for source in range(f...  49.6 us
    psum x1, blocking collectives, body(): grad_total = grad_total + lax.psum(partial_value, ('seg', 'samp'))  37.7 us
    ppermute x16, waiting for transfers between devices, shifted(): lax.ppermute(value, axis, [(source, source + steps) for source in range(f...  29.1 us
    dot_general x8, matrix products, stiffness(): jnp.einsum('sjb,jab->sja', field_round, rigidity_diagonal_cells, preferre...  11.7 us
    dot_general x8, matrix products, blockwise(): jnp.einsum('jab,sjb->sja', inverse_diagonal_cells, field_round, preferred...  10.8 us
    gather x8, local copies, waits for them, and re-layouts, stiffness(): jnp.take(interfaces, joined_segment_table[0], axis=1).astype(jnp.float32)  9.89 us
    dot_general x8, matrix products, stiffness(): jnp.einsum('sjb,jab->sja', lower_field, rigidity_lower_cells, preferred_e...  9.36 us
  transfers between devices with their start and end apart: 16, of which 8 were waited for; matrix products, arithmetic and copies ran while one was open for 4% of the time, Pallas kernels for 0%

commit v1 on v0

v1 whole, which is shorter than its diff:
```python
import functools
import math

import jax
import jax.numpy as jnp
from jax import lax
from jax.experimental import pallas as pl
from jax.experimental.pallas import tpu as pltpu
from jax.sharding import PartitionSpec as P

STEPS = 4
EXCHANGES = 2 * STEPS - 1
GROUP = 6
F32 = jnp.float32
BF16 = jnp.bfloat16
MESH = pl.DeviceIdType.MESH


def dot_nt(left, right):
    return lax.dot_general(left, right, (((1,), (1,)), ((), ())), preferred_element_type=F32)


def dot_nn(left, right):
    return lax.dot_general(left, right, (((1,), (0,)), ((), ())), preferred_element_type=F32)


def kernel(
    segments,
    halves,
    diag_hbm,
    lower_hbm,
    inverse_hbm,
    bed_ref,
    regime_ref,
    push_ref,
    shape_ref,
    weight_ref,
    table_ref,
    joint_ref,
    x_ref,
    grad_ref,
    diag,
    lower,
    inverse,
    load,
    res,
    step_field,
    tangent,
    x_round,
    step_round,
    sample_sum,
    inverse_push,
    edge,
    below,
    partials,
    local_sem,
    send_sem,
    recv_sem,
    edge_send,
    edge_recv,
    cell_sem,
    sum_sem,
    *gathered,
):
    blocks = diag.shape[0]
    samples, width = load.shape[1], load.shape[2]
    me = lax.axis_index("seg")
    core = lax.axis_index("samp")
    devices = segments * halves
    flat = me * halves + core
    after = lax.rem(me + 1, segments)
    before = lax.rem(me + segments - 1, segments)

    barrier = pltpu.get_barrier_semaphore()

    def greet(k, carry):
        t = lax.rem(flat + k, devices)
        pl.semaphore_signal(
            barrier, inc=1, device_id=(t // halves, lax.rem(t, halves)), device_id_type=MESH
        )
        return carry

    lax.fori_loop(1, devices, greet, 0)

    loads = [
        pltpu.make_async_copy(inverse_hbm, inverse, local_sem.at[0]),
        pltpu.make_async_copy(diag_hbm, diag, local_sem.at[1]),
        pltpu.make_async_copy(lower_hbm, lower.at[pl.ds(0, blocks)], local_sem.at[2]),
    ]
    for copy in loads:
        copy.start()

    temperature = dot_nt(weight_ref[...], shape_ref[...])
    for j in range(blocks):
        load[j] = temperature[:, j : j + 1] * push_ref[j : j + 1, :]
    sample_sum[...] = jnp.zeros_like(sample_sum)

    def post(e, first_value, last_value):
        gathered[e][me] = first_value
        edge[e] = last_value

        def send(k, carry):
            pltpu.make_async_remote_copy(
                src_ref=gathered[e].at[me],
                dst_ref=gathered[e].at[me],
                send_sem=send_sem.at[e],
                recv_sem=recv_sem.at[e],
                device_id=(lax.rem(me + k, segments), core),
                device_id_type=MESH,
            ).start()
            return carry

        pltpu.make_async_remote_copy(
            src_ref=edge.at[e],
            dst_ref=below.at[e],
            send_sem=edge_send.at[e],
            recv_sem=edge_recv.at[e],
            device_id=(after, core),
            device_id_type=MESH,
        ).start()
        lax.fori_loop(1, segments, send, 0)

    def arrived(e):
        others = gathered[e].at[pl.ds(0, segments - 1)]
        pltpu.make_async_copy(others, others, recv_sem.at[e]).wait()
        pltpu.make_async_copy(below.at[e], below.at[e], edge_recv.at[e]).wait()

    def sent(e):
        others = gathered[e].at[pl.ds(0, segments - 1)]
        pltpu.make_async_copy(others, others, send_sem.at[e]).wait()
        pltpu.make_async_copy(edge.at[e], edge.at[e], edge_send.at[e]).wait()

    def stiff(low, own, high, j):
        pair = jnp.concatenate([low, own], axis=1)
        cells = jnp.concatenate([lower[j], diag[j]], axis=1)
        return dot_nt(pair, cells) + dot_nn(high, lower[j + 1])

    def spring(e, own):
        own = own.astype(F32)
        total = jnp.zeros_like(own)
        for l in range(table_ref.shape[1]):
            partner = gathered[e][table_ref[0, l]].astype(F32)
            total = total + joint_ref[0, l] * (own - partner)
        return total

    def ends(e, field):
        first_value, last_value = field[0], field[blocks - 1]
        low = stiff(below[e], first_value, field[1], 0) + spring(e, first_value)
        high = stiff(field[blocks - 2], last_value, gathered[e][after], blocks - 1)
        return low, high

    def ballast(x, j):
        k = bed_ref[pl.ds(j, 1), :]
        code = jnp.full(x.shape, regime_ref[j], jnp.int32)
        fraction = 1.0 / (1.0 + jnp.abs(x))
        slide = jnp.tanh(x)
        unit = jnp.where(code == 0, x, jnp.where(code == 1, x * fraction, slide))
        slope = jnp.where(
            code == 0, 1.0, jnp.where(code == 1, fraction * fraction, 1.0 - slide * slide)
        )
        return k * unit, k * slope

    def precondition(j, value):
        return dot_nt(value.astype(BF16), inverse[j])

    def finish_first(j, kx):
        force, slope = ballast(x_ref[j], j)
        residual = load[j] - kx - force
        first = precondition(j, residual)
        res[j] = residual
        tangent[j] = slope
        step_field[j] = first
        step_round[j] = first.astype(BF16)

    def finish_second(j, kf, start):
        first = step_field[j]
        if start:
            second = load[j] - kf - bed_ref[pl.ds(j, 1), :] * first
            x = first + precondition(j, second)
        else:
            second = res[j] - kf - tangent[j] * first
            x = x_ref[j] + first + precondition(j, second)
        rounded = x.astype(BF16)
        x_ref[j] = x
        x_round[j] = rounded
        sample_sum[pl.ds(j, 1), :] += jnp.sum(rounded.astype(F32), axis=0, keepdims=True)

    def every(start, stop, work):
        count = (stop - start) // GROUP

        def group(i, carry):
            for u in range(GROUP):
                work(start + i * GROUP + u)
            return carry

        lax.fori_loop(0, count, group, 0)
        for j in range(start + count * GROUP, stop):
            work(j)

    def start_first(j):
        first = precondition(j, load[j])
        step_field[j] = first
        step_round[j] = first.astype(BF16)

    loads[0].wait()
    start_first(0)
    start_first(blocks - 1)
    pl.semaphore_wait(barrier, devices - 1)
    post(0, step_round[0], step_round[blocks - 1])
    cell = pltpu.make_async_remote_copy(
        src_ref=lower_hbm.at[0],
        dst_ref=lower.at[blocks],
        send_sem=cell_sem.at[0],
        recv_sem=cell_sem.at[1],
        device_id=(before, core),
        device_id_type=MESH,
    )
    cell.start()
    every(1, blocks - 1, start_first)

    def push_product(j):
        push = push_ref[pl.ds(j, 1), :]
        high = push.astype(BF16)
        rest = push - high.astype(F32)
        middle = rest.astype(BF16)
        low = (rest - middle.astype(F32)).astype(BF16)
        rows = jnp.concatenate(
            [jnp.broadcast_to(part, (16, width)) for part in (high, middle, low)], axis=0
        )
        product = dot_nt(rows, inverse[j])
        inverse_push[pl.ds(j, 1), :] = product[0:1] + product[16:17] + product[32:33]

    every(0, blocks, push_product)
    loads[1].wait()
    loads[2].wait()

    def interior_first(j):
        finish_first(j, stiff(x_round[j - 1], x_round[j], x_round[j + 1], j))

    for step in range(STEPS):
        if step > 0:
            e = 2 * step - 1
            every(1, blocks - 1, interior_first)
            arrived(e)
            low, high = ends(e, x_round)
            finish_first(0, low)
            finish_first(blocks - 1, high)
            post(e + 1, step_round[0], step_round[blocks - 1])
        e = 2 * step

        def interior_second(j):
            kf = stiff(step_round[j - 1], step_round[j], step_round[j + 1], j)
            finish_second(j, kf, step == 0)

        every(1, blocks - 1, interior_second)
        arrived(e)
        if step == 0:
            cell.wait()
            lower[0] = jnp.where(jnp.full((width, width), me, jnp.int32) > 0, lower[0].astype(F32), 0.0).astype(BF16)
            lower[blocks] = jnp.where(
                jnp.full((width, width), me, jnp.int32) < segments - 1, lower[blocks].astype(F32), 0.0
            ).astype(BF16)
        low, high = ends(e, step_round)
        finish_second(0, low, step == 0)
        finish_second(blocks - 1, high, step == 0)
        if step < STEPS - 1:
            post(e + 1, x_round[0], x_round[blocks - 1])

    weighted = jnp.sum(inverse_push[...] * sample_sum[...], axis=1, keepdims=True)
    partials[flat] = jnp.sum(shape_ref[...].astype(F32) * weighted, axis=0, keepdims=True)

    def share(k, carry):
        t = lax.rem(flat + k, devices)
        pltpu.make_async_remote_copy(
            src_ref=partials.at[flat],
            dst_ref=partials.at[flat],
            send_sem=sum_sem.at[0],
            recv_sem=sum_sem.at[1],
            device_id=(t // halves, lax.rem(t, halves)),
            device_id_type=MESH,
        ).start()
        return carry

    lax.fori_loop(1, devices, share, 0)
    for e in range(EXCHANGES):
        sent(e)
    others = partials.at[pl.ds(0, devices - 1)]
    pltpu.make_async_copy(others, others, sum_sem.at[1]).wait()
    grad_ref[...] = jnp.sum(partials[...], axis=0)
    pltpu.make_async_copy(others, others, sum_sem.at[0]).wait()


def body(segments, halves, *arguments):
    (diag, lower, inverse, bed, regime, push, shapes, weights, table, joint) = arguments
    samples = weights.shape[0]
    blocks, width = diag.shape[0], diag.shape[1]
    terms = shapes.shape[1]
    devices = segments * halves
    vmem = pl.BlockSpec(memory_space=pltpu.VMEM)
    smem = pl.BlockSpec(memory_space=pltpu.SMEM)
    anywhere = pl.BlockSpec(memory_space=pltpu.HBM)
    field = (blocks, samples, width)
    rim = (EXCHANGES, samples, width)
    x, grad = pl.pallas_call(
        functools.partial(kernel, segments, halves),
        out_shape=(
            jax.ShapeDtypeStruct(field, F32),
            jax.ShapeDtypeStruct((1, terms), F32),
        ),
        in_specs=[anywhere, anywhere, anywhere, vmem, smem, vmem, vmem, vmem, smem, smem],
        out_specs=(vmem, vmem),
        scratch_shapes=[
            pltpu.VMEM((blocks, width, width), BF16),
            pltpu.VMEM((blocks + 1, width, width), BF16),
            pltpu.VMEM((blocks, width, width), BF16),
            pltpu.VMEM(field, F32),
            pltpu.VMEM(field, F32),
            pltpu.VMEM(field, F32),
            pltpu.VMEM(field, F32),
            pltpu.VMEM(field, BF16),
            pltpu.VMEM(field, BF16),
            pltpu.VMEM((blocks, width), F32),
            pltpu.VMEM((blocks, width), F32),
            pltpu.VMEM(rim, BF16),
            pltpu.VMEM(rim, BF16),
            pltpu.VMEM((devices, 1, terms), F32),
            pltpu.SemaphoreType.DMA((3,)),
            pltpu.SemaphoreType.DMA((EXCHANGES,)),
            pltpu.SemaphoreType.DMA((EXCHANGES,)),
            pltpu.SemaphoreType.DMA((EXCHANGES,)),
            pltpu.SemaphoreType.DMA((EXCHANGES,)),
            pltpu.SemaphoreType.DMA((2,)),
            pltpu.SemaphoreType.DMA((2,)),
        ]
        + [pltpu.VMEM((segments, samples, width), BF16)] * EXCHANGES,
        compiler_params=pltpu.CompilerParams(
            collective_id=0, has_side_effects=True, vmem_limit_bytes=40 * 1024 * 1024
        ),
    )(diag, lower, inverse, bed, regime, push, shapes, weights, table, joint)
    scale = math.sqrt(terms / (blocks * segments * samples * halves * width))
    return jnp.transpose(x, (1, 0, 2)), grad[0] * scale


def solution(mesh):
    placed = (
        P("seg", None, None),
        P("seg", None, None),
        P("seg", None, None),
        P("seg", None),
        P("seg"),
        P("seg", None),
        P("seg", None),
        P("samp", None),
        P("seg", None),
        P("seg", None),
    )
    return jax.shard_map(
        functools.partial(body, mesh.shape["seg"], mesh.shape["samp"]),
        mesh=mesh,
        in_specs=placed,
        out_specs=(P("samp", "seg", None), P()),
        check_vma=False,
    )
```

time: 462 us -> 66.9 us (0.14)
  blocking collectives: 307 us -> 0 us
  Pallas kernels: 0 us -> 55.5 us
  starting transfers between devices: 49.6 us -> 0 us
  matrix products: 43.6 us -> 0 us
  waiting for transfers between devices: 29.1 us -> 0 us
  local copies, waits for them, and re-layouts: 22.6 us -> 9.68 us
  other arithmetic: 5.63 us -> 0.58 us
    all_gather x7 -> x0, blocking collectives: 270 us -> none  [stiffness(): lax.all_gather(field_round[:, :1, :], 'seg', axis=1, tiled=True)]
    pallas_call x0 -> x1, Pallas kernels: none -> 55.5 us  [body(): pl.pallas_call(functools.partial(kernel, segments, halves), out_shape=(ja...]
    ppermute x16 -> x0, starting transfers between devices: 49.6 us -> none  [shifted(): lax.ppermute(value, axis, [(source, source + steps) for source in range(f...]
    dot_general x41 -> x0, matrix products: 43.6 us -> none  [the longest x8 11.7 us: stiffness(): jnp.einsum('sjb,jab->sja', field_round, rigidity_diagonal_cells, preferre...]
    psum x1 -> x0, blocking collectives: 37.7 us -> none  [body(): grad_total = grad_total + lax.psum(partial_value, ('seg', 'samp'))]
    ppermute x16 -> x0, waiting for transfers between devices: 29.1 us -> none  [shifted(): lax.ppermute(value, axis, [(source, source + steps) for source in range(f...]
    gather x8 -> x0, local copies, waits for them, and re-layouts: 9.89 us -> none  [stiffness(): jnp.take(interfaces, joined_segment_table[0], axis=1).astype(jnp.float32)]
    slice x33 -> x0, local copies, waits for them, and re-layouts: 5.08 us -> none  [the longest x8 4.89 us: stiffness(): above_rim = shifted(upward[:, :1, :], 'seg', -1)]
  transfers between devices with their start and end apart: 16 -> 0, of which waited for: 8 -> 0; matrix products, arithmetic and copies ran while one was open for 4% -> 0% of each run, Pallas kernels for 0% -> 0%
where the time goes in v1:
time: 66.9 us; the launch traced here: 66.4 us
  Pallas kernels  55.5 us (83%)
  local copies, waits for them, and re-layouts  9.68 us (14%)
    pallas_call x1, Pallas kernels, body(): pl.pallas_call(functools.partial(kernel, segments, halves), out_shape=(ja...  55.5 us
    unnamed x21, local copies, waits for them, and re-layouts  9.68 us

profile of v1, /device:TPU:0, one launch (start us, length us, event | category | flops | bytes accessed | tf_op | source)
XLA Modules:
  0.0 66.4 jit_solution(2066319846231519620)
XLA Ops:
  0.6 0.0 copy-start
  0.6 1.2 %copy-done = bf16[32,128,128]{2,1,0:T(8,128)(2,1)S(1)} copy-done((bf16[32,128,128]{2,1,0:T(8,128)(2,1)S(1)}, bf16[32,128,128]{2,1,0:T(8,128)(2,1)}, u32[]{:S(2)}) %copy-start) | copy-done | bytes 1048600
  1.9 0.0 copy-start.1
  1.9 1.2 %copy-done.1 = bf16[32,128,128]{2,1,0:T(8,128)(2,1)S(1)} copy-done((bf16[32,128,128]{2,1,0:T(8,128)(2,1)S(1)}, bf16[32,128,128]{2,1,0:T(8,128)(2,1)}, u32[]{:S(2)}) %copy-start.1) | copy-done | bytes 1048600
  3.1 0.0 copy-start.2
  3.1 1.2 %copy-done.2 = bf16[32,128,128]{2,1,0:T(8,128)(2,1)S(1)} copy-done((bf16[32,128,128]{2,1,0:T(8,128)(2,1)S(1)}, bf16[32,128,128]{2,1,0:T(8,128)(2,1)}, u32[]{:S(2)}) %copy-start.2) | copy-done | bytes 1048600
  4.3 0.0 copy-start.3
  4.3 0.8 %copy-done.3 = bf16[32,512]{1,0:T(8,128)(2,1)S(1)} copy-done((bf16[32,512]{1,0:T(8,128)(2,1)S(1)}, bf16[32,512]{1,0:T(8,128)(2,1)}, u32[]{:S(2)}) %copy-start.3) | copy-done | bytes 32792
  5.1 0.0 copy-start.4
  5.1 0.8 %copy-done.4 = bf16[32,512]{1,0:T(8,128)(2,1)S(1)} copy-done((bf16[32,512]{1,0:T(8,128)(2,1)S(1)}, bf16[32,512]{1,0:T(8,128)(2,1)}, u32[]{:S(2)}) %copy-start.4) | copy-done | bytes 32792
  5.8 0.0 copy-start.5
  5.8 0.7 %copy-done.5 = f32[32,128]{1,0:T(8,128)S(1)} copy-done((f32[32,128]{1,0:T(8,128)S(1)}, f32[32,128]{1,0:T(8,128)}, u32[]{:S(2)}) %copy-start.5) | copy-done | bytes 16408
  6.5 0.0 copy-start.6
  6.5 0.7 %copy-done.6 = f32[32,128]{1,0:T(8,128)S(1)} copy-done((f32[32,128]{1,0:T(8,128)S(1)}, f32[32,128]{1,0:T(8,128)}, u32[]{:S(2)}) %copy-start.6) | copy-done | bytes 16408
  7.3 0.0 copy-start.7
  7.3 0.7 copy-done.7
  7.9 0.0 copy-start.8
  7.9 0.7 copy-done.8
  8.6 0.0 copy-start.9
  8.6 0.7 copy-done.9
  9.2 55.5 %shard_map.113 = (f32[32,32,128]{2,1,0:T(8,128)S(1)}, f32[1,512]{1,0:T(1,128)S(1)}) custom-call(bf16[32,128,128]{2,1,0:T(8,128)(2,1)S(1)} %copy-done, bf16[32,128,128]{2,1,0:T(8,128)(2,1)S(1)} %copy-done.1, bf16[32,128,128]{2,1,0:T(8,128)(2,1)S(1)} %copy-done.2, f32[32,128]{1,0:T(8,128)S(1)} %copy-done.5, s32[32]{0:T(128)S(1)} %copy-done.7, ...), custom_call_target="tpu_custom_call" | custom-call | tf_op jit(solution)/shard_map/pallas_call | solution.py:304
  64.7 1.1 %copy.12 = f32[32,32,128]{2,1,0:T(8,128)} copy(f32[32,32,128]{2,0,1:T(8,128)S(1)} %bitcast.2) | data formatting | bytes 1048576
  65.8 0.6 broadcast_multiply_fusion
Async XLA Ops:
  0.6 1.2 %copy-start = (bf16[32,128,128]{2,1,0:T(8,128)(2,1)S(1)}, bf16[32,128,128]{2,1,0:T(8,128)(2,1)}, u32[]{:S(2)}) copy-start(bf16[32,128,128]{2,1,0:T(8,128)(2,1)} %diag_hbm.1) | copy-start | bytes 3145732
  1.9 1.2 %copy-start.1 = (bf16[32,128,128]{2,1,0:T(8,128)(2,1)S(1)}, bf16[32,128,128]{2,1,0:T(8,128)(2,1)}, u32[]{:S(2)}) copy-start(bf16[32,128,128]{2,1,0:T(8,128)(2,1)} %lower_hbm.1) | copy-start | bytes 3145732
  3.1 1.2 %copy-start.2 = (bf16[32,128,128]{2,1,0:T(8,128)(2,1)S(1)}, bf16[32,128,128]{2,1,0:T(8,128)(2,1)}, u32[]{:S(2)}) copy-start(bf16[32,128,128]{2,1,0:T(8,128)(2,1)} %inverse_hbm.1) | copy-start | bytes 3145732
  4.3 0.8 %copy-start.3 = (bf16[32,512]{1,0:T(8,128)(2,1)S(1)}, bf16[32,512]{1,0:T(8,128)(2,1)}, u32[]{:S(2)}) copy-start(bf16[32,512]{1,0:T(8,128)(2,1)} %shape_ref.1) | copy-start | bytes 98308
  5.1 0.8 %copy-start.4 = (bf16[32,512]{1,0:T(8,128)(2,1)S(1)}, bf16[32,512]{1,0:T(8,128)(2,1)}, u32[]{:S(2)}) copy-start(bf16[32,512]{1,0:T(8,128)(2,1)} %weight_ref.1) | copy-start | bytes 98308
  5.8 0.7 %copy-start.5 = (f32[32,128]{1,0:T(8,128)S(1)}, f32[32,128]{1,0:T(8,128)}, u32[]{:S(2)}) copy-start(f32[32,128]{1,0:T(8,128)} %bed_ref.1) | copy-start | bytes 49156
  6.5 0.7 %copy-start.6 = (f32[32,128]{1,0:T(8,128)S(1)}, f32[32,128]{1,0:T(8,128)}, u32[]{:S(2)}) copy-start(f32[32,128]{1,0:T(8,128)} %push_ref.1) | copy-start | bytes 49156
  7.3 0.7 copy-start.7
  7.9 0.7 copy-start.8
  8.6 0.7 copy-start.9

commit v2 on v1

v2 whole, which is shorter than its diff:
```python
import functools
import math

import jax
import jax.numpy as jnp
from jax import lax
from jax.experimental import pallas as pl
from jax.experimental.pallas import tpu as pltpu
from jax.sharding import PartitionSpec as P

STEPS = 4
EXCHANGES = 2 * STEPS - 1
GROUP = 10
F32 = jnp.float32
BF16 = jnp.bfloat16
MESH = pl.DeviceIdType.MESH


def dot_nt(left, right):
    return lax.dot_general(left, right, (((1,), (1,)), ((), ())), preferred_element_type=F32)


def dot_nn(left, right):
    return lax.dot_general(left, right, (((1,), (0,)), ((), ())), preferred_element_type=F32)


def kernel(
    segments,
    halves,
    diag_hbm,
    lower_hbm,
    inverse_hbm,
    bed_hbm,
    regime_ref,
    push_hbm,
    shape_hbm,
    weight_hbm,
    table_ref,
    joint_ref,
    x_hbm,
    grad_ref,
    diag,
    lower,
    inverse,
    bed_ref,
    push_ref,
    shape_ref,
    weight_ref,
    load,
    res,
    step_field,
    tangent,
    x_round,
    step_round,
    sample_sum,
    inverse_push,
    edge,
    below,
    partials,
    pair,
    x_ref,
    local_sem,
    send_sem,
    recv_sem,
    edge_send,
    edge_recv,
    cell_sem,
    sum_sem,
    *gathered,
):
    blocks = diag.shape[0]
    samples, width = load.shape[1], load.shape[2]
    me = lax.axis_index("seg")
    core = lax.axis_index("samp")
    after = lax.rem(me + 1, segments)
    before = lax.rem(me + segments - 1, segments)
    peers = segments + halves - 2

    barrier = pltpu.get_barrier_semaphore()

    def greet(k, carry):
        pl.semaphore_signal(
            barrier, inc=1, device_id=(lax.rem(me + k, segments), core), device_id_type=MESH
        )
        return carry

    def greet_half(k, carry):
        pl.semaphore_signal(
            barrier, inc=1, device_id=(me, lax.rem(core + k, halves)), device_id_type=MESH
        )
        return carry

    loads = [
        pltpu.make_async_copy(weight_hbm, weight_ref, local_sem.at[3]),
        pltpu.make_async_copy(shape_hbm, shape_ref, local_sem.at[4]),
        pltpu.make_async_copy(push_hbm, push_ref, local_sem.at[5]),
        pltpu.make_async_copy(bed_hbm, bed_ref, local_sem.at[6]),
        pltpu.make_async_copy(inverse_hbm, inverse, local_sem.at[0]),
        pltpu.make_async_copy(diag_hbm, diag, local_sem.at[1]),
        pltpu.make_async_copy(lower_hbm, lower.at[pl.ds(0, blocks)], local_sem.at[2]),
    ]
    for copy in loads:
        copy.start()
    lax.fori_loop(1, segments, greet, 0)
    lax.fori_loop(1, halves, greet_half, 0)
    for copy in loads[:4]:
        copy.wait()

    temperature = dot_nt(weight_ref[...], shape_ref[...])
    for j in range(blocks):
        load[j] = temperature[:, j : j + 1] * push_ref[j : j + 1, :]
    sample_sum[...] = jnp.zeros_like(sample_sum)

    def partner(k):
        return me ^ k if segments & (segments - 1) == 0 else lax.rem(me + k, segments)

    def post(e, first_value, last_value):
        gathered[e][me] = first_value
        edge[e] = last_value

        def send(k, carry):
            pltpu.make_async_remote_copy(
                src_ref=gathered[e].at[me],
                dst_ref=gathered[e].at[me],
                send_sem=send_sem.at[e],
                recv_sem=recv_sem.at[e],
                device_id=(partner(segments - k), core),
                device_id_type=MESH,
            ).start()
            return carry

        pltpu.make_async_remote_copy(
            src_ref=edge.at[e],
            dst_ref=below.at[e],
            send_sem=edge_send.at[e],
            recv_sem=edge_recv.at[e],
            device_id=(after, core),
            device_id_type=MESH,
        ).start()
        lax.fori_loop(1, segments, send, 0)

    def arrived(e):
        others = gathered[e].at[pl.ds(0, segments - 1)]
        pltpu.make_async_copy(others, others, recv_sem.at[e]).wait()
        pltpu.make_async_copy(below.at[e], below.at[e], edge_recv.at[e]).wait()

    def sent(e):
        others = gathered[e].at[pl.ds(0, segments - 1)]
        pltpu.make_async_copy(others, others, send_sem.at[e]).wait()
        pltpu.make_async_copy(edge.at[e], edge.at[e], edge_send.at[e]).wait()

    def stiff(low, own, high, j):
        pair = jnp.concatenate([low, own], axis=1)
        cells = jnp.concatenate([lower[j], diag[j]], axis=1)
        return dot_nt(pair, cells) + dot_nn(high, lower[j + 1])

    def spring(e, own):
        own = own.astype(F32)
        total = jnp.zeros_like(own)
        for l in range(table_ref.shape[1]):
            partner = gathered[e][table_ref[0, l]].astype(F32)
            total = total + joint_ref[0, l] * (own - partner)
        return total

    def ends_before(field):
        low = dot_nt(field[0], diag[0]) + dot_nn(field[1], lower[1])
        pair_cells = jnp.concatenate([lower[blocks - 1], diag[blocks - 1]], axis=1)
        high = dot_nt(jnp.concatenate([field[blocks - 2], field[blocks - 1]], axis=1), pair_cells)
        return low, high

    def ends_after(e, field, known):
        low = known[0] + dot_nt(below[e], lower[0]) + spring(e, field[0])
        high = known[1] + dot_nn(gathered[e][after], lower[blocks])
        return [low, high]

    def ballast(x, j):
        k = bed_ref[pl.ds(j, 1), :]
        code = jnp.full(x.shape, regime_ref[j], jnp.int32)
        fraction = 1.0 / (1.0 + jnp.abs(x))
        slide = jnp.tanh(x)
        unit = jnp.where(code == 0, x, jnp.where(code == 1, x * fraction, slide))
        slope = jnp.where(
            code == 0, 1.0, jnp.where(code == 1, fraction * fraction, 1.0 - slide * slide)
        )
        return k * unit, k * slope

    def precondition(j, value):
        return dot_nt(value.astype(BF16), inverse[j])

    def finish_first(js, kxs, pairs=None):
        if pairs is None:
            pairs = [ballast(x_ref[j], j) for j in js]
        residuals = [load[j] - kx - pair[0] for j, kx, pair in zip(js, kxs, pairs)]
        firsts = [precondition(j, residual) for j, residual in zip(js, residuals)]
        for j, residual, pair, first in zip(js, residuals, pairs, firsts):
            res[j] = residual
            tangent[j] = pair[1]
            step_field[j] = first
            step_round[j] = first.astype(BF16)

    def finish_second(js, kfs, start):
        firsts = [step_field[j] for j in js]
        if start:
            seconds = [
                load[j] - kf - bed_ref[pl.ds(j, 1), :] * first
                for j, kf, first in zip(js, kfs, firsts)
            ]
            xs = firsts
        else:
            seconds = [
                res[j] - kf - tangent[j] * first for j, kf, first in zip(js, kfs, firsts)
            ]
            xs = [x_ref[j] + first for j, first in zip(js, firsts)]
        xs = [x + precondition(j, second) for j, x, second in zip(js, xs, seconds)]
        rounds = [x.astype(BF16) for x in xs]
        sums = [jnp.sum(rounded.astype(F32), axis=0, keepdims=True) for rounded in rounds]
        for j, x, rounded, total in zip(js, xs, rounds, sums):
            x_ref[j] = x
            x_round[j] = rounded
            sample_sum[pl.ds(j, 1), :] += total

    def every(start, stop, work):
        count = (stop - start) // GROUP

        def group(i, carry):
            work([start + i * GROUP + u for u in range(GROUP)])
            return carry

        lax.fori_loop(0, count, group, 0)
        if start + count * GROUP < stop:
            work(list(range(start + count * GROUP, stop)))

    def start_first(js):
        firsts = [precondition(j, load[j]) for j in js]
        for j, first in zip(js, firsts):
            step_field[j] = first
            step_round[j] = first.astype(BF16)

    loads[4].wait()
    start_first([0, blocks - 1])
    pl.semaphore_wait(barrier, peers)
    post(0, step_round[0], step_round[blocks - 1])
    cell = pltpu.make_async_remote_copy(
        src_ref=lower_hbm.at[0],
        dst_ref=lower.at[blocks],
        send_sem=cell_sem.at[0],
        recv_sem=cell_sem.at[1],
        device_id=(before, core),
        device_id_type=MESH,
    )
    cell.start()
    every(1, blocks - 1, start_first)

    def push_product(js):
        products = []
        for j in js:
            push = push_ref[pl.ds(j, 1), :]
            high = push.astype(BF16)
            rest = push - high.astype(F32)
            middle = rest.astype(BF16)
            low = (rest - middle.astype(F32)).astype(BF16)
            rows = jnp.concatenate(
                [jnp.broadcast_to(part, (16, width)) for part in (high, middle, low)], axis=0
            )
            products.append(dot_nt(rows, inverse[j]))
        for j, product in zip(js, products):
            inverse_push[pl.ds(j, 1), :] = product[0:1] + product[16:17] + product[32:33]

    every(0, blocks, push_product)
    loads[5].wait()
    loads[6].wait()

    def inner(field, js):
        values = [field[js[0] - 1 + u] for u in range(len(js) + 2)]
        return [stiff(values[u], values[u + 1], values[u + 2], j) for u, j in enumerate(js)]

    def interior_first(js):
        finish_first(js, inner(x_round, js))

    for step in range(STEPS):
        if step > 0:
            e = 2 * step - 1
            every(1, blocks - 1, interior_first)
            known = ends_before(x_round)
            pairs = [ballast(x_ref[j], j) for j in (0, blocks - 1)]
            arrived(e)
            finish_first([0, blocks - 1], ends_after(e, x_round, known), pairs)
            post(e + 1, step_round[0], step_round[blocks - 1])
        e = 2 * step

        def interior_second(js):
            finish_second(js, inner(step_round, js), step == 0)

        every(1, blocks - 1, interior_second)
        known = ends_before(step_round)
        arrived(e)
        if step == 0:
            cell.wait()
            lower[0] = jnp.where(jnp.full((width, width), me, jnp.int32) > 0, lower[0].astype(F32), 0.0).astype(BF16)
            lower[blocks] = jnp.where(
                jnp.full((width, width), me, jnp.int32) < segments - 1, lower[blocks].astype(F32), 0.0
            ).astype(BF16)
        finish_second([0, blocks - 1], ends_after(e, step_round, known), step == 0)
        if step < STEPS - 1:
            post(e + 1, x_round[0], x_round[blocks - 1])

    weighted = jnp.sum(inverse_push[...] * sample_sum[...], axis=1, keepdims=True)
    pair[core] = jnp.sum(shape_ref[...].astype(F32) * weighted, axis=0, keepdims=True)

    def share_half(k, carry):
        pltpu.make_async_remote_copy(
            src_ref=pair.at[core],
            dst_ref=pair.at[core],
            send_sem=sum_sem.at[2],
            recv_sem=sum_sem.at[3],
            device_id=(me, lax.rem(core + k, halves)),
            device_id_type=MESH,
        ).start()
        return carry

    def share(k, carry):
        pltpu.make_async_remote_copy(
            src_ref=partials.at[me],
            dst_ref=partials.at[me],
            send_sem=sum_sem.at[0],
            recv_sem=sum_sem.at[1],
            device_id=(lax.rem(me + k, segments), core),
            device_id_type=MESH,
        ).start()
        return carry

    lax.fori_loop(1, halves, share_half, 0)
    result = pltpu.make_async_copy(x_ref, x_hbm, local_sem.at[7])
    result.start()
    other_half = pair.at[pl.ds(0, halves - 1)]
    pltpu.make_async_copy(other_half, other_half, sum_sem.at[3]).wait()
    partials[me] = jnp.sum(pair[...], axis=0)
    lax.fori_loop(1, segments, share, 0)
    for e in range(EXCHANGES):
        sent(e)
    pltpu.make_async_copy(other_half, other_half, sum_sem.at[2]).wait()
    result.wait()
    others = partials.at[pl.ds(0, segments - 1)]
    pltpu.make_async_copy(others, others, sum_sem.at[1]).wait()
    grad_ref[...] = jnp.sum(partials[...], axis=0)
    pltpu.make_async_copy(others, others, sum_sem.at[0]).wait()


def body(segments, halves, *arguments):
    (diag, lower, inverse, bed, regime, push, shapes, weights, table, joint) = arguments
    samples = weights.shape[0]
    blocks, width = diag.shape[0], diag.shape[1]
    terms = shapes.shape[1]
    vmem = pl.BlockSpec(memory_space=pltpu.VMEM)
    smem = pl.BlockSpec(memory_space=pltpu.SMEM)
    anywhere = pl.BlockSpec(memory_space=pltpu.HBM)
    field = (blocks, samples, width)
    rim = (EXCHANGES, samples, width)
    x, grad = pl.pallas_call(
        functools.partial(kernel, segments, halves),
        out_shape=(
            jax.ShapeDtypeStruct(field, F32),
            jax.ShapeDtypeStruct((1, terms), F32),
        ),
        in_specs=[anywhere, anywhere, anywhere, anywhere, smem, anywhere, anywhere, anywhere, smem, smem],
        out_specs=(anywhere, vmem),
        scratch_shapes=[
            pltpu.VMEM((blocks, width, width), BF16),
            pltpu.VMEM((blocks + 1, width, width), BF16),
            pltpu.VMEM((blocks, width, width), BF16),
            pltpu.VMEM(bed.shape, bed.dtype),
            pltpu.VMEM(push.shape, push.dtype),
            pltpu.VMEM(shapes.shape, shapes.dtype),
            pltpu.VMEM(weights.shape, weights.dtype),
            pltpu.VMEM(field, F32),
            pltpu.VMEM(field, F32),
            pltpu.VMEM(field, F32),
            pltpu.VMEM(field, F32),
            pltpu.VMEM(field, BF16),
            pltpu.VMEM(field, BF16),
            pltpu.VMEM((blocks, width), F32),
            pltpu.VMEM((blocks, width), F32),
            pltpu.VMEM(rim, BF16),
            pltpu.VMEM(rim, BF16),
            pltpu.VMEM((segments, 1, terms), F32),
            pltpu.VMEM((halves, 1, terms), F32),
            pltpu.VMEM(field, F32),
            pltpu.SemaphoreType.DMA((8,)),
            pltpu.SemaphoreType.DMA((EXCHANGES,)),
            pltpu.SemaphoreType.DMA((EXCHANGES,)),
            pltpu.SemaphoreType.DMA((EXCHANGES,)),
            pltpu.SemaphoreType.DMA((EXCHANGES,)),
            pltpu.SemaphoreType.DMA((2,)),
            pltpu.SemaphoreType.DMA((4,)),
        ]
        + [pltpu.VMEM((segments, samples, width), BF16)] * EXCHANGES,
        compiler_params=pltpu.CompilerParams(
            collective_id=0, has_side_effects=True, vmem_limit_bytes=63 * 1024 * 1024
        ),
    )(diag, lower, inverse, bed, regime, push, shapes, weights, table, joint)
    scale = math.sqrt(terms / (blocks * segments * samples * halves * width))
    return jnp.transpose(x, (1, 0, 2)), grad[0] * scale


def solution(mesh):
    placed = (
        P("seg", None, None),
        P("seg", None, None),
        P("seg", None, None),
        P("seg", None),
        P("seg"),
        P("seg", None),
        P("seg", None),
        P("samp", None),
        P("seg", None),
        P("seg", None),
    )
    return jax.shard_map(
        functools.partial(body, mesh.shape["seg"], mesh.shape["samp"]),
        mesh=mesh,
        in_specs=placed,
        out_specs=(P("samp", "seg", None), P()),
        check_vma=False,
    )
```

time: 66.9 us -> 55.5 us (0.83)
  local copies, waits for them, and re-layouts: 9.68 us -> 2.15 us
  Pallas kernels: 55.5 us -> 51.9 us
    unnamed x21 -> x3, local copies, waits for them, and re-layouts: 9.68 us -> 2.15 us
    pallas_call x1, Pallas kernels: 55.5 us -> 51.9 us  [body(): pl.pallas_call(functools.partial(kernel, segments, halves), out_shape=(ja...]
where the time goes in v2:
time: 55.5 us; the launch traced here: 55.3 us
  Pallas kernels  51.9 us (94%)
  local copies, waits for them, and re-layouts  2.15 us (4%)
  between operations  0.65 us (1%)
  other arithmetic  0.58 us (1%)
    pallas_call x1, Pallas kernels, body(): pl.pallas_call(functools.partial(kernel, segments, halves), out_shape=(ja...  51.9 us
    unnamed x3, local copies, waits for them, and re-layouts  2.15 us

profile of v2, /device:TPU:0, one launch (start us, length us, event | category | flops | bytes accessed | tf_op | source)
XLA Modules:
  0.0 55.3 jit_solution(182143449226351061)
XLA Ops:
  0.6 51.9 %shard_map.113 = (f32[32,32,128]{2,1,0:T(8,128)}, f32[1,512]{1,0:T(1,128)}) custom-call(bf16[32,128,128]{2,1,0:T(8,128)(2,1)} %diag_hbm.1, bf16[32,128,128]{2,1,0:T(8,128)(2,1)} %lower_hbm.1, bf16[32,128,128]{2,1,0:T(8,128)(2,1)} %inverse_hbm.1, f32[32,128]{1,0:T(8,128)} %bed_hbm.1, s32[32]{0:T(128)} %regime_ref.1, f32[32,128]{1,0:T(8,128)} %push_hbm.1, ...), custom_call_target="tpu_custom_call" | custom-call | tf_op jit(solution)/shard_map/pallas_call | solution.py:359
  52.6 0.0 copy-start
  52.6 2.1 %copy.12 = f32[32,32,128]{2,1,0:T(8,128)} copy(f32[32,32,128]{2,0,1:T(8,128)} %bitcast.2) | data formatting | bytes 1048576
  54.7 0.0 copy-done
  54.7 0.6 %broadcast_multiply_fusion = f32[1,512]{1,0:T(1,128)} fusion(f32[1,512]{1,0:T(1,128)S(1)} %copy-done), kind=kLoop, calls=%fused_computation | loop fusion | flops 512 | bytes 4096 | tf_op jit(solution)/shard_map/mul | solution.py:402
Async XLA Ops:
  52.6 2.2 %copy-start = (f32[1,512]{1,0:T(1,128)S(1)}, f32[1,512]{1,0:T(1,128)}, u32[]{:S(2)}) copy-start(f32[1,512]{1,0:T(1,128)} %get-tuple-element.5) | copy-start | bytes 6148

commit v3 on v2

--- a/solution.py
+++ b/solution.py
@@ -59,6 +59,7 @@
     partials,
     pair,
     x_ref,
+    turned,
     local_sem,
     send_sem,
     recv_sem,
@@ -95,20 +96,32 @@
         pltpu.make_async_copy(shape_hbm, shape_ref, local_sem.at[4]),
         pltpu.make_async_copy(push_hbm, push_ref, local_sem.at[5]),
         pltpu.make_async_copy(bed_hbm, bed_ref, local_sem.at[6]),
-        pltpu.make_async_copy(inverse_hbm, inverse, local_sem.at[0]),
+        pltpu.make_async_copy(
+            inverse_hbm.at[pl.ds(1, blocks - 2)],
+            inverse.at[pl.ds(1, blocks - 2)],
+            local_sem.at[0],
+        ),
         pltpu.make_async_copy(diag_hbm, diag, local_sem.at[1]),
         pltpu.make_async_copy(lower_hbm, lower.at[pl.ds(0, blocks)], local_sem.at[2]),
     ]
-    for copy in loads:
+    end_loads = [
+        pltpu.make_async_copy(inverse_hbm.at[j], inverse.at[j], local_sem.at[sem])
+        for j, sem in ((0, 8), (blocks - 1, 9))
+    ]
+    for copy in loads[:3] + end_loads + loads[3:]:
         copy.start()
     lax.fori_loop(1, segments, greet, 0)
     lax.fori_loop(1, halves, greet_half, 0)
-    for copy in loads[:4]:
+    for copy in loads[:3]:
         copy.wait()
 
     temperature = dot_nt(weight_ref[...], shape_ref[...])
-    for j in range(blocks):
+
+    def set_load(j):
         load[j] = temperature[:, j : j + 1] * push_ref[j : j + 1, :]
+
+    set_load(0)
+    set_load(blocks - 1)
     sample_sum[...] = jnp.zeros_like(sample_sum)
 
     def partner(k):
@@ -169,7 +182,7 @@
         return low, high
 
     def ends_after(e, field, known):
-        low = known[0] + dot_nt(below[e], lower[0]) + spring(e, field[0])
+        low = known[0] + dot_nn(below[e], turned[2]) + spring(e, field[0])
         high = known[1] + dot_nn(gathered[e][after], lower[blocks])
         return [low, high]
 
@@ -185,7 +198,10 @@
         return k * unit, k * slope
 
     def precondition(j, value):
-        return dot_nt(value.astype(BF16), inverse[j])
+        value = value.astype(BF16)
+        if isinstance(j, int) and j in (0, blocks - 1):
+            return dot_nn(value, turned[0 if j == 0 else 1])
+        return dot_nt(value, inverse[j])
 
     def finish_first(js, kxs, pairs=None):
         if pairs is None:
@@ -231,12 +247,13 @@
             work(list(range(start + count * GROUP, stop)))
 
     def start_first(js):
-        firsts = [precondition(j, load[j]) for j in js]
+        firsts = [dot_nt(load[j].astype(BF16), inverse[j]) for j in js]
         for j, first in zip(js, firsts):
             step_field[j] = first
             step_round[j] = first.astype(BF16)
 
-    loads[4].wait()
+    for copy in end_loads:
+        copy.wait()
     start_first([0, blocks - 1])
     pl.semaphore_wait(barrier, peers)
     post(0, step_round[0], step_round[blocks - 1])
@@ -249,6 +266,10 @@
         device_id_type=MESH,
     )
     cell.start()
+    for j in range(1, blocks - 1):
+        set_load(j)
+    loads[3].wait()
+    loads[4].wait()
     every(1, blocks - 1, start_first)
 
     def push_product(js):
@@ -269,6 +290,10 @@
     every(0, blocks, push_product)
     loads[5].wait()
     loads[6].wait()
+    turned[0] = inverse[0].astype(F32).T.astype(BF16)
+    turned[1] = inverse[blocks - 1].astype(F32).T.astype(BF16)
+    has_before = jnp.full((width, width), me, jnp.int32) > 0
+    turned[2] = jnp.where(has_before, lower[0].astype(F32).T, 0.0).astype(BF16)
 
     def inner(field, js):
         values = [field[js[0] - 1 + u] for u in range(len(js) + 2)]
@@ -296,7 +321,6 @@
         arrived(e)
         if step == 0:
             cell.wait()
-            lower[0] = jnp.where(jnp.full((width, width), me, jnp.int32) > 0, lower[0].astype(F32), 0.0).astype(BF16)
             lower[blocks] = jnp.where(
                 jnp.full((width, width), me, jnp.int32) < segments - 1, lower[blocks].astype(F32), 0.0
             ).astype(BF16)
@@ -385,7 +409,8 @@
             pltpu.VMEM((segments, 1, terms), F32),
             pltpu.VMEM((halves, 1, terms), F32),
             pltpu.VMEM(field, F32),
-            pltpu.SemaphoreType.DMA((8,)),
+            pltpu.VMEM((3, width, width), BF16),
+            pltpu.SemaphoreType.DMA((10,)),
             pltpu.SemaphoreType.DMA((EXCHANGES,)),
             pltpu.SemaphoreType.DMA((EXCHANGES,)),
             pltpu.SemaphoreType.DMA((EXCHANGES,)),

time: 55.5 us -> 54.6 us (0.984)
  Pallas kernels: 51.9 us -> 51.1 us
    pallas_call x1, Pallas kernels: 51.9 us -> 51.1 us  [body(): pl.pallas_call(functools.partial(kernel, segments, halves), out_shape=(ja...]
where the time goes in v3:
time: 54.6 us; the launch traced here: 54.5 us
  Pallas kernels  51.1 us (94%)
  local copies, waits for them, and re-layouts  2.15 us (4%)
  between operations  0.65 us (1%)
  other arithmetic  0.58 us (1%)
    pallas_call x1, Pallas kernels, body(): pl.pallas_call(functools.partial(kernel, segments, halves), out_shape=(ja...  51.1 us
    unnamed x3, local copies, waits for them, and re-layouts  2.15 us

profile of v3, /device:TPU:0, one launch (start us, length us, event | category | flops | bytes accessed | tf_op | source)
XLA Modules:
  0.0 54.5 jit_solution(7419739523513054095)
XLA Ops:
  0.6 51.1 %shard_map.113 = (f32[32,32,128]{2,1,0:T(8,128)}, f32[1,512]{1,0:T(1,128)}) custom-call(bf16[32,128,128]{2,1,0:T(8,128)(2,1)} %diag_hbm.1, bf16[32,128,128]{2,1,0:T(8,128)(2,1)} %lower_hbm.1, bf16[32,128,128]{2,1,0:T(8,128)(2,1)} %inverse_hbm.1, f32[32,128]{1,0:T(8,128)} %bed_hbm.1, s32[32]{0:T(128)} %regime_ref.1, f32[32,128]{1,0:T(8,128)} %push_hbm.1, ...), custom_call_target="tpu_custom_call" | custom-call | tf_op jit(solution)/shard_map/pallas_call | solution.py:383
  51.7 0.0 copy-start
  51.8 2.1 %copy.12 = f32[32,32,128]{2,1,0:T(8,128)} copy(f32[32,32,128]{2,0,1:T(8,128)} %bitcast.2) | data formatting | bytes 1048576
  53.9 0.0 copy-done
  53.9 0.6 %broadcast_multiply_fusion = f32[1,512]{1,0:T(1,128)} fusion(f32[1,512]{1,0:T(1,128)S(1)} %copy-done), kind=kLoop, calls=%fused_computation | loop fusion | flops 512 | bytes 4096 | tf_op jit(solution)/shard_map/mul | solution.py:427
Async XLA Ops:
  51.7 2.2 %copy-start = (f32[1,512]{1,0:T(1,128)S(1)}, f32[1,512]{1,0:T(1,128)}, u32[]{:S(2)}) copy-start(f32[1,512]{1,0:T(1,128)} %get-tuple-element.5) | copy-start | bytes 6148

commit v4 on v3

--- a/solution.py
+++ b/solution.py
@@ -127,6 +127,13 @@
     def partner(k):
         return me ^ k if segments & (segments - 1) == 0 else lax.rem(me + k, segments)
 
+    def mask(k):
+        if segments % 4:
+            return k
+        half, quarter = segments // 2, segments // 4
+        crossed = segments - 1 - (k - 1) // 2 - lax.rem(k - 1, 2) * quarter
+        return jnp.where(k <= half, crossed, segments - k)
+
     def post(e, first_value, last_value):
         gathered[e][me] = first_value
         edge[e] = last_value
@@ -137,7 +144,7 @@
                 dst_ref=gathered[e].at[me],
                 send_sem=send_sem.at[e],
                 recv_sem=recv_sem.at[e],
-                device_id=(partner(segments - k), core),
+                device_id=(partner(mask(k)), core),
                 device_id_type=MESH,
             ).start()
             return carry

time: 54.6 us -> 53.7 us (0.984)
  Pallas kernels: 51.1 us -> 50.2 us
    pallas_call x1, Pallas kernels: 51.1 us -> 50.2 us  [body(): pl.pallas_call(functools.partial(kernel, segments, halves), out_shape=(ja...]
where the time goes in v4:
time: 53.7 us; the launch traced here: 53.6 us
  Pallas kernels  50.2 us (93%)
  local copies, waits for them, and re-layouts  2.15 us (4%)
  between operations  0.65 us (1%)
  other arithmetic  0.58 us (1%)
    pallas_call x1, Pallas kernels, body(): pl.pallas_call(functools.partial(kernel, segments, halves), out_shape=(ja...  50.2 us
    unnamed x3, local copies, waits for them, and re-layouts  2.15 us

profile of v4, /device:TPU:0, one launch (start us, length us, event | category | flops | bytes accessed | tf_op | source)
XLA Modules:
  0.0 53.6 jit_solution(17611203647723296824)
XLA Ops:
  0.6 50.2 %shard_map.113 = (f32[32,32,128]{2,1,0:T(8,128)}, f32[1,512]{1,0:T(1,128)}) custom-call(bf16[32,128,128]{2,1,0:T(8,128)(2,1)} %diag_hbm.1, bf16[32,128,128]{2,1,0:T(8,128)(2,1)} %lower_hbm.1, bf16[32,128,128]{2,1,0:T(8,128)(2,1)} %inverse_hbm.1, f32[32,128]{1,0:T(8,128)} %bed_hbm.1, s32[32]{0:T(128)} %regime_ref.1, f32[32,128]{1,0:T(8,128)} %push_hbm.1, ...), custom_call_target="tpu_custom_call" | custom-call | tf_op jit(solution)/shard_map/pallas_call | solution.py:390
  50.8 0.0 copy-start
  50.8 2.1 %copy.12 = f32[32,32,128]{2,1,0:T(8,128)} copy(f32[32,32,128]{2,0,1:T(8,128)} %bitcast.2) | data formatting | bytes 1048576
  53.0 0.0 copy-done
  53.0 0.6 %broadcast_multiply_fusion = f32[1,512]{1,0:T(1,128)} fusion(f32[1,512]{1,0:T(1,128)S(1)} %copy-done), kind=kLoop, calls=%fused_computation | loop fusion | flops 512 | bytes 4096 | tf_op jit(solution)/shard_map/mul | solution.py:434
Async XLA Ops:
  50.8 2.2 %copy-start = (f32[1,512]{1,0:T(1,128)S(1)}, f32[1,512]{1,0:T(1,128)}, u32[]{:S(2)}) copy-start(f32[1,512]{1,0:T(1,128)} %get-tuple-element.5) | copy-start | bytes 6148
